TPU v7x, 32 devices: a whole 2x2x4 slice. The times are simulated.
32 devices in a mesh: seq: 16 (over z, y, core), chan: 2 (over x).
Axes of the slice: x: 2, y: 2, z: 4, core: 2. Of those that a mesh axis runs over, the one named last changes fastest.
Arguments:
- tokens: bfloat16 [2, 4096, 1536], P(None, 'seq'), may hold values from -6 to 6
- gain_mix: float32 [1536], replicated, may hold values from 0.25 to 1.75
- w_in: bfloat16 [3, 1536, 1536], P(None, None, 'chan'), may hold values from -0.15625 to 0.15625
- kernel: float32 [3, 1536], P(None, 'chan'), may hold values from -3 to 3
- w_out: bfloat16 [1536, 1536], P('chan'), may hold values from -0.15625 to 0.15625
- gain_ffn: float32 [1536], replicated, may hold values from 0.25 to 1.75
- w_gate: bfloat16 [1536, 6912], P(None, 'chan'), may hold values from -0.15625 to 0.15625
- w_up: bfloat16 [1536, 6912], P(None, 'chan'), may hold values from -0.15625 to 0.15625
- w_down: bfloat16 [6912, 1536], P('chan'), may hold values from -0.078125 to 0.078125
- cotangent: bfloat16 [2, 4096, 1536], P(None, 'seq'), may hold values from -6 to 6
Outputs:
- block_out: bfloat16 [2, 4096, 1536], P(None, 'seq')
- d_tokens: bfloat16 [2, 4096, 1536], P(None, 'seq')
- g_gain_mix: float32 [1536], P('seq')
- g_w_in: float32 [3, 1536, 1536], P(None, 'seq', 'chan')
- g_kernel: float32 [3, 2, 768], P(None, 'chan', 'seq')
- g_w_out: float32 [1536, 1536], P('chan', 'seq')
- g_gain_ffn: float32 [1536], P('seq')
- g_w_gate: float32 [1536, 6912], P('seq', 'chan')
- g_w_up: float32 [1536, 6912], P('seq', 'chan')
- g_w_down: float32 [6912, 1536], P('chan', 'seq')
All inputs are finite; a program needn't handle non-finite values.
Results may differ from a plain program's by a relative error of at most 0.017.
Values may be sent and summed in bfloat16 or wider, within the bound.
A program may use at most 320 MiB of HBM per device.

v0:
```python
import functools

import jax
import jax.numpy as jnp
from jax import lax
from jax.experimental import pallas as pl
from jax.experimental.pallas import tpu as pltpu
from jax.sharding import PartitionSpec as P

epsilon = 1e-05
BF = jnp.bfloat16
F32 = jnp.float32
MESH = pl.DeviceIdType.MESH
LANE = 128
NZ = 4
ROWS_CHUNK = 128
ZF_COLS = 1152


def nn(a, b):
    return jnp.dot(a, b, preferred_element_type=F32)


def tn(a, b):
    return lax.dot_general(a, b, (((0,), (0,)), ((), ())), preferred_element_type=F32)


def nt(a, b):
    return lax.dot_general(a, b, (((1,), (1,)), ((), ())), preferred_element_type=F32)


def inv_rms(v):
    return lax.rsqrt(jnp.mean(v * v, axis=-1, keepdims=True) + epsilon)


class Take:
    def __init__(self, limit):
        self.used, self.limit = 0, limit

    def __call__(self, count=1):
        base = self.used
        self.used += count
        assert self.used <= self.limit
        return base


N_SEND, N_RECV, N_LOCAL = 128, 192, 64

SCHEDULE = {
    "dhA": (("end", (1, 0)), ("mid", (0, 2)),),
    "dnD": (("mid", (0, 0)),),
    "nb0": (("end", (3, 0)), ("end", (1, 2)), ("end", (2, 1)),),
    "nb1": (("mid", (0, 1)), ("mid", (3, 0)),),
    "cb": (("end", (2, 0)), ("mid", "pair"),),
    "tail": (("end", (3, 1)), ("mid", (2, 2)), ("mid", (1, 0)),),
    "gc2": (("mid", (2, 0)), ("mid", (1, 1)), ("mid", (3, 1)),),
    "gc3": (("mid", (1, 2)), ("mid", (3, 2)),),
    "blk1": (("end", (1, 1)),),
    "blk3": (("mid", (2, 1)), ("mid", "pair sum"), ("mid", (4, 0)), ("mid", (1, 3)), ("mid", (4, 2)),),
    "dt0": (("end", (4, 0)), ("end", (4, 1)), ("end", (3, 2)), ("end", (2, 2)), ("end", (1, 3)),),
    "dt1": (("end", "pair"), ("mid", (4, 1)), ("mid", (2, 3)),),
    "dt3": (("end", (4, 2)), ("end", (2, 3)), ("end", (3, 3)), ("mid", (3, 3)),),
    "sm": (("end", (4, 3)), ("end", "pair sum"), ("mid", (4, 3)),),
}


def step_kernel(
    dims,
    tokens, gain_mix_hbm, w_in, taps_hbm, w_out, gain_ffn_hbm, w_gate, w_up, w_down, cot,
    block_out, d_tokens, g_ffn, g_conv, small_out,
    gb0, gb1, gb2, gb3, gb4, yb0, yb1, yb2, yb3, yb4, zb0, zb1, zb2, zb3, zb4,
    cr_dh, cr_dn,
    gain_mix, taps, gain_ffn, tok_v, wg_v, wu_v, wd_v, dy_v, h2_v, h1_v, hid, dg, du, pb, pc, px, bx, gated, resid, gall,
    ring, xr_dh, xr_dn, xr_d1, rb, ld, outs, halo_s, halo_r, dhalo_s, dhalo_r, tail, pb_tail, px_tail,
    sm, sm_r, ss, rs, ls,
):
    R, T, D, CL, FL, FW = dims
    S = R // T
    CH = CL // 2
    GR = D // NZ
    SR = GR // 2
    DR = SR // 2
    NCH = R // ROWS_CHUNK
    take_s, take_r, take_l = Take(N_SEND), Take(N_RECV), Take(N_LOCAL)

    s = lax.axis_index("seq")
    x = lax.axis_index("chan")
    n_seq = 4 * NZ
    z, y, c = s // 4, (s // 2) % 2, s % 2

    def did(z_, y_, c_):
        return ((z_ * 2 + y_) * 2 + c_, x)

    core_dev = did(z, y, 1 - c)
    y_dev = did(z, 1 - y, c)
    x_dev = (s, 1 - x)
    mid = jnp.logical_and(z > 0, z < NZ - 1)
    end = jnp.logical_not(mid)

    def remote(src, dst, si, ri, dev):
        return pltpu.make_async_remote_copy(
            src_ref=src, dst_ref=dst, send_sem=ss.at[si], recv_sem=rs.at[ri],
            device_id=dev, device_id_type=MESH,
        )

    def wait_recv(dst, ri):
        remote(dst, dst, 0, ri, core_dev).wait_recv()

    def wait_send(src, si):
        remote(src, src, si, 0, core_dev).wait_send()

    def local(src, dst, li):
        return pltpu.make_async_copy(src, dst, ls.at[li])

    l_tok, l_win, l_wout, l_dy, l_small = take_l(), take_l(3), take_l(), take_l(), take_l(3)
    ld_tok = local(tokens, tok_v, l_tok)
    ld_tok.start()
    win_views = [wg_v.at[:, pl.ds(0, CL)], wg_v.at[:, pl.ds(CL, CL)], wu_v.at[:, pl.ds(0, CL)]]
    wout_view = wd_v.at[pl.ds(pl.multiple_of(x * CL, CL), CL), :]

    def load_w_in():
        return [local(w_in.at[m], win_views[m], l_win + m) for m in range(3)]

    for cp in load_w_in():
        cp.start()
    ld_small = [
        local(src, dst, l_small + i)
        for i, (src, dst) in enumerate(
            ((gain_mix_hbm, gain_mix), (taps_hbm, taps), (gain_ffn_hbm, gain_ffn))
        )
    ]
    for cp in ld_small:
        cp.start()
    ld_wout = local(w_out, wout_view, l_wout)
    ld_wout.start()
    ld_dy = local(cot, dy_v.at[0], l_dy)

    bar = pltpu.get_barrier_semaphore()

    def greet(dev):
        pl.semaphore_signal(bar, inc=1, device_id=dev, device_id_type=MESH)

    greet(core_dev)
    greet(x_dev)
    others = [(k, did((z + k // 2) % NZ, (y + k % 2) % 2, c)) for k in range(1, 2 * NZ)]
    for _, dev in others:
        greet(dev)
    has_prev = s > 0
    has_next = s < n_seq - 1
    prev_dev = ((s + n_seq - 1) % n_seq, x)
    next_dev = ((s + 1) % n_seq, x)
    greet(prev_dev)
    greet(next_dev)
    pl.semaphore_wait(bar, 3 + 2 * NZ)

    QR, SUBS = CL // 4, 4
    PR = QR // SUBS
    s_w, r_w = [take_s(SUBS) for _ in range(4)], [take_r(SUBS) for _ in range(4)]

    def w_rows(half, quarter, sub):
        return wd_v.at[pl.ds(pl.multiple_of(half * CL + quarter * QR + sub * PR, PR), PR), :]

    mine_q, pair_q = y * 2 + c, (1 - y) * 2 + c
    core_q, far_q = y * 2 + (1 - c), (1 - y) * 2 + (1 - c)

    def w_over_x(sub):
        src = w_out.at[pl.ds(pl.multiple_of(mine_q * QR + sub * PR, PR), PR), :]
        return remote(src, w_rows(x, mine_q, sub), s_w[0] + sub, r_w[0] + sub, x_dev)

    def w_over_y(sub):
        ref = w_rows(1 - x, mine_q, sub)
        return remote(ref, ref, s_w[1] + sub, r_w[1] + sub, y_dev)

    def w_over_core(sub):
        ref = w_rows(1 - x, mine_q, sub)
        return remote(ref, ref, s_w[2] + sub, r_w[2] + sub, core_dev)

    def w_far_over_core(sub):
        ref = w_rows(1 - x, pair_q, sub)
        return remote(ref, ref, s_w[3] + sub, r_w[3] + sub, core_dev)

    def w_pass_on(sub):
        wait_recv(w_rows(1 - x, mine_q, sub), r_w[0] + sub)
        w_over_y(sub).start()
        w_over_core(sub).start()

    def w_pass_far(sub):
        wait_recv(w_rows(1 - x, pair_q, sub), r_w[1] + sub)
        w_far_over_core(sub).start()

    for sub in range(SUBS):
        w_over_x(sub).start()

    l_w = take_l(3)
    win_start = pl.multiple_of(c * (FL - FW), LANE)
    ld_wg = local(w_gate.at[:, pl.ds(win_start, FW)], wg_v, l_w)
    ld_wu = local(w_up.at[:, pl.ds(win_start, FW)], wu_v, l_w + 1)
    ld_wd = local(w_down.at[pl.ds(win_start, FW), :], wd_v, l_w + 2)

    sm[...] = jnp.zeros_like(sm)
    for cp in ld_small:
        cp.wait()
    gain_mix_row = gain_mix[...].reshape(1, D)
    gain_ffn_row = gain_ffn[...].reshape(1, D)
    k_taps = [taps[t : t + 1, :] for t in range(3)]

    ld_tok.wait()

    CPS = T // ROWS_CHUNK
    NC = CL // 256
    s_h1, r_h1 = take_s(S), take_r(S)
    s_ha, r_ha = take_s(S), take_r(S)
    s_mx, r_mx = take_s(NCH), take_r(NCH)
    row_iota = lax.broadcasted_iota(jnp.int32, (T, 256), 0)
    top_iota = row_iota[0:16]

    def conv_terms(now, h, iota):
        h14 = jnp.broadcast_to(h[14:15], now.shape)
        h15 = jnp.broadcast_to(h[15:16], now.shape)
        one = jnp.where(iota == 0, h15, pltpu.roll(now, 1, 0))
        two = jnp.where(iota == 0, h14, jnp.where(iota == 1, h15, pltpu.roll(now, 2, 0)))
        return now, one, two

    def tap_cols(cols):
        return [taps[t : t + 1, cols] for t in range(3)]

    def convolve(terms, cols):
        now, one, two = terms
        k0, k1, k2 = tap_cols(cols)
        return k0 * two + k1 * one + k2 * now

    def h1_send(q):
        rows = pl.ds(q * T, T)
        return remote(h1_v.at[0, rows], h1_v.at[1, rows], s_h1 + q, r_h1 + q, core_dev)

    def halo_send(q):
        return remote(halo_s.at[q], halo_r.at[q], s_ha + q, r_ha + q, next_dev)

    own_cols = pl.ds(pl.multiple_of(x * CL, CL), CL)
    other_cols = pl.ds(pl.multiple_of((1 - x) * CL, CL), CL)

    def gated_send(k):
        ref = gall.at[k, :, own_cols]
        return remote(ref, ref, s_mx + k, r_mx + k, x_dev)

    def mixer_out(k):
        gall[k, :, own_cols] = gated[k * ROWS_CHUNK : (k + 1) * ROWS_CHUNK, :]
        gated_send(k).start()

    for q in range(S):
        rows = pl.ds(q * T, T)

        def norm_rows(k, _, q=q):
            chunk = pl.ds(pl.multiple_of(q * T + k * ROWS_CHUNK, ROWS_CHUNK), ROWS_CHUNK)
            xv = tok_v[chunk, :].astype(F32)
            h1_v[0, chunk, :] = (xv * inv_rms(xv) * gain_mix_row).astype(BF)
            return 0

        lax.fori_loop(0, CPS, norm_rows, 0)
        if q > 0:
            w_pass_on(1)
        if q == 0:
            for cp in load_w_in():
                cp.wait()

        def in_proj(j, _, q=q, rows=rows):
            cols = pl.ds(pl.multiple_of(j * 256, 256), 256)
            cols1 = pl.ds(pl.multiple_of(CL + j * 256, 256), 256)
            h = h1_v[0, rows, :]
            b = nn(h, wg_v[:, cols])
            pb[rows, cols] = b.astype(BF)
            xx = nn(h, wu_v[:, cols])
            px[rows, cols] = xx.astype(BF)
            inner = (b * xx).astype(BF)
            bx[rows, cols] = inner
            halo_s[q, :, cols] = inner[T - 16 : T]
            pcv = nn(h, wg_v[:, cols1])
            pc[rows, cols] = pcv.astype(BF)
            now = inner.astype(F32)
            cv = convolve(conv_terms(now, jnp.zeros_like(now[0:16]), row_iota), cols)
            gated[rows, cols] = (pcv * cv).astype(BF)
            return 0

        lax.fori_loop(0, NC, in_proj, 0)
        if q == S - 1:
            ld_wg.start()
            ld_wu.start()

        @pl.when(has_next)
        def _(q=q):
            halo_send(q).start()

        for k in range(CPS - 1, 0, -1):
            mixer_out(q * CPS + k)
        if q == 0:
            w_pass_on(0)
        else:
            w_pass_on(2)
            w_pass_far(0)

        @pl.when(has_prev)
        def _(q=q):
            wait_recv(halo_r.at[q], r_ha + q)

        @pl.when(jnp.logical_not(has_prev))
        def _(q=q):
            halo_r[q] = jnp.zeros_like(halo_r[q])

        def conv_top(j, _, q=q):
            cols = pl.ds(pl.multiple_of(j * 256, 256), 256)
            top = pl.ds(q * T, 16)
            now = bx[top, cols].astype(F32)
            cv = convolve(conv_terms(now, halo_r[q, :, cols].astype(F32), top_iota), cols)
            gated[top, cols] = (pc[top, cols].astype(F32) * cv).astype(BF)
            return 0

        lax.fori_loop(0, NC, conv_top, 0)
        mixer_out(q * CPS)
        h1_send(q).start()
        if q == 0:
            ld_dy.start()
            s_dy, r_dy = take_s(), take_r()
            send_dy = remote(cot, dy_v.at[1], s_dy, r_dy, core_dev)
            send_dy.start()
    w_pass_on(3)
    w_pass_far(1)

    s_h2, r_h2 = take_s(NCH), take_r(NCH)
    ld_wg.wait()
    ld_wu.wait()
    NF = FW // 256
    overlap = 2 * FW - FL
    col_iota = lax.broadcasted_iota(jnp.int32, (2 * ROWS_CHUNK, 256), 1)

    def sent(n):
        return (n // CPS) * CPS + (CPS - 1 - n % CPS)

    def residual_chunk(k):
        rows = pl.ds(pl.multiple_of(k * ROWS_CHUNK, ROWS_CHUNK), ROWS_CHUNK)
        wait_recv(gall.at[k, :, other_cols], r_mx + k)

        def out_tile(j, _):
            cols = pl.ds(pl.multiple_of(j * 512, 512), 512)
            resid[rows, cols] = tok_v[rows, cols].astype(F32) + nn(gall[k], wd_v[0 : 2 * CL, cols])
            return 0

        lax.fori_loop(0, D // 512, out_tile, 0, unroll=True)
        res = resid[rows, :]
        h2_v[0, rows, :] = (res * inv_rms(res) * gain_ffn_row).astype(BF)
        remote(h2_v.at[0, rows], h2_v.at[1, rows], s_h2 + k, r_h2 + k, core_dev).start()

    def forward_chunk(k):
        rows = pl.ds(pl.multiple_of(k * ROWS_CHUNK, ROWS_CHUNK), ROWS_CHUNK)
        wait_recv(h2_v.at[1, rows], r_h2 + k)

        def tile(j, _):
            cols = pl.ds(pl.multiple_of(j * 256, 256), 256)
            h = h2_v[:, rows, :].reshape(2 * ROWS_CHUNK, D)
            g = nn(h, wg_v[:, cols])
            u = nn(h, wu_v[:, cols])
            keep = col_iota + j * 256 >= c * overlap
            sg = jax.nn.sigmoid(g)
            si = jnp.where(keep, g * sg, 0.0)
            shape = (2, ROWS_CHUNK, 256)
            hid[:, rows, cols] = (si * u).astype(BF).reshape(shape)
            slope = jnp.where(keep, u * sg * (1.0 + g * (1.0 - sg)), 0.0)
            dg[:, rows, cols] = slope.astype(BF).reshape(shape)
            du[:, rows, cols] = si.astype(BF).reshape(shape)
            return 0

        lax.fori_loop(0, NF, tile, 0, unroll=True)

    w_pass_far(2)
    w_pass_far(3)
    ld_wout.wait()
    for sub in range(SUBS):
        wait_recv(w_rows(1 - x, core_q, sub), r_w[2] + sub)
        wait_recv(w_rows(1 - x, far_q, sub), r_w[3] + sub)
    residual_chunk(sent(0))

    def chunk_loop(n, _):
        @pl.when(n + 1 < NCH)
        def _():
            residual_chunk(sent(n + 1))

        forward_chunk(sent(n))
        return 0

    lax.fori_loop(0, NCH, chunk_loop, 0)
    for sub in range(SUBS):
        w_over_x(sub).wait_send()
        for send in (w_over_y, w_over_core, w_far_over_core):
            send(sub).wait_send()
    ld_wd.start()
    ld_dy.wait()
    send_dy.wait()
    for k in range(NCH):
        gated_send(k).wait_send()
        wait_send(h2_v.at[0, pl.ds(k * ROWS_CHUNK, ROWS_CHUNK)], s_h2 + k)

    gbs = [gb0, gb1, gb2, gb3, gb4]
    ybs = [yb0, yb1, yb2, yb3, yb4]
    zbs = [zb0, zb1, zb2, zb3, zb4]
    widths = [ZF_COLS, FW - ZF_COLS, FW, FW, 2 * CL]
    s_y = [None] + [take_s(NZ) for _ in range(4)]
    r_y = [None] + [take_r(NZ) for _ in range(4)]
    s_z = [take_s(2 * NZ)] + [take_s(NZ) for _ in range(4)]
    r_z = [take_r(4 * NZ)] + [take_r(2 * NZ) for _ in range(4)]

    def order(e):
        if e == NZ - 1:
            return z
        per_z = {0: (3, 2, 1), 1: (3, 0, 2), 2: (0, 3, 1), 3: (0, 1, 2)}
        v = per_z[3][e]
        for zz in range(3):
            v = jnp.where(z == zz, per_z[zz][e], v)
        return v

    def order_dyn(u):
        v = order(NZ - 1)
        for e in range(NZ - 1):
            v = jnp.where(u == e, order(e), v)
        return v

    def per_core(j, act):
        if j in (1, 4):
            act(lambda ref: ref)
            return

        @pl.when(c == 0)
        def _():
            act(lambda ref: ref)

        @pl.when(c == 1)
        def _():
            act(lambda ref: ref.at[:, pl.ds(overlap, widths[j] - overlap)])

    def z_send(j, src, e, zp, h=None):
        to_right = zp > z
        d = jnp.where(to_right, 0, 1)
        dev = did(jnp.clip(jnp.where(to_right, z + 1, z - 1), 0, NZ - 1), y, c)
        if h is None:
            dst, si, ri = zbs[j].at[d, zp], s_z[j] + e, r_z[j] + d * NZ + zp
        else:
            dst, si, ri = zbs[j].at[d, zp, h], s_z[j] + 2 * e + h, r_z[j] + (d * NZ + zp) * 2 + h
        per_core(j, lambda cut: remote(cut(src), cut(dst), si, ri, dev).start())

    l_g = take_l(12)

    def y_send(j, u):
        zp = order_dyn(u) if not isinstance(u, int) else order(u)
        src, dst = gbs[j].at[zp, 1 - y], ybs[j].at[zp]
        per_core(j, lambda cut: remote(cut(src), cut(dst), s_y[j] + u, r_y[j] + u, y_dev).start())

    def g_block(lhs_ref, rhs_ref, zp, pair, parts=(0, 1)):
        lhs = lhs_ref[:, :, pl.ds(pl.multiple_of(zp * GR, GR), GR)].reshape(2 * R, GR)
        cut = -(-FW // 512) * 256
        for n in parts:
            cols = slice(0, cut) if n == 0 else slice(cut, FW)
            v = tn(lhs, rhs_ref[:, :, cols].reshape(2 * R, cols.stop - cols.start)).astype(BF)
            outs[2 * pair, :, cols] = v[:SR]
            outs[2 * pair + 1, :, cols] = v[SR:]

    def down_copies(zp, pair):
        return [
            cp
            for h in range(2)
            for cp in (
                local(outs.at[2 * pair + h, :, pl.ds(0, ZF_COLS)], gb0.at[zp, h], l_g + 4 * pair + 2 * h),
                local(
                    outs.at[2 * pair + h, :, pl.ds(ZF_COLS, FW - ZF_COLS)],
                    gb1.at[zp, h], l_g + 4 * pair + 2 * h + 1,
                ),
            )
        ]

    def down_sends(u):
        zp = order(u)
        for cp in down_copies(zp, u % 2):
            cp.wait()
        if u < NZ - 1:

            @pl.when(end)
            def _():
                for h in range(2):
                    z_send(0, gb0.at[zp, h], u, zp, h)

            y_send(1, u)

    for u in range(NZ):
        g_block(dy_v, hid, order(u), u % 2, (0,))
        if u > 0:
            down_sends(u - 1)
        g_block(dy_v, hid, order(u), u % 2, (1,))
        for cp in down_copies(order(u), u % 2):
            cp.start()
    down_sends(NZ - 1)

    ld_wd.wait()

    def hid_back(slot, _):
        for j in range(NF):
            cols = slice(j * 256, (j + 1) * 256)
            dh = nt(dy_v[slot], wd_v[cols, :])
            dg[slot, :, cols] = (dh * dg[slot, :, cols].astype(F32)).astype(BF)
            du[slot, :, cols] = (dh * du[slot, :, cols].astype(F32)).astype(BF)
        return 0

    lax.fori_loop(0, 2, hid_back, 0)

    def plain_copies(gb, zp, pair):
        return [local(outs.at[2 * pair + h], gb.at[zp, h], l_g + 2 * pair + h) for h in range(2)]

    def gate_up(u, _):
        zp = order_dyn(u)

        def up_sends(u):
            for cp in plain_copies(gb3, order_dyn(u), 1):
                cp.wait()

            @pl.when(u < 2)
            def _():
                y_send(3, u)

        g_block(h2_v, dg, zp, 0, (0,))

        @pl.when(u > 0)
        def _():
            up_sends(u - 1)

        g_block(h2_v, dg, zp, 0, (1,))
        for cp in plain_copies(gb2, zp, 0):
            cp.start()
        g_block(h2_v, du, zp, 1, (0,))
        for cp in plain_copies(gb2, zp, 0):
            cp.wait()

        @pl.when(u < 3)
        def _():
            y_send(2, u)

        g_block(h2_v, du, zp, 1, (1,))
        for cp in plain_copies(gb3, zp, 1):
            cp.start()
        return 0

    lax.fori_loop(0, NZ, gate_up, 0)
    for cp in plain_copies(gb3, order(NZ - 1), 1):
        cp.wait()

    l_e = take_l(4)
    is_role = {"end": end, "mid": mid}
    slot_last = {role: [None] * outs.shape[0] for role in is_role}
    slot_next = {role: 0 for role in is_role}

    def claim_slot(role):
        o = slot_next[role]
        slot_next[role] = (o + 1) % outs.shape[0]
        if slot_last[role][o] is not None:
            slot_last[role][o]()
            slot_last[role][o] = None
        return o

    ADD_ROWS = 32

    def add_into(dst, srcs):
        def rows_add(k, _):
            rows = pl.ds(pl.multiple_of(k * ADD_ROWS, ADD_ROWS), ADD_ROWS)
            acc = srcs[0][rows, :].astype(F32)
            for src in srcs[1:]:
                acc = acc + src[rows, :].astype(F32)
            dst[rows, :] = acc.astype(BF)
            return 0

        lax.fori_loop(0, SR // ADD_ROWS, rows_add, 0)

    def fetch(j, srcs):
        w = widths[j]
        views, copies = [], []
        for i, (src, ri) in enumerate(srcs):
            if ri is not None:
                per_core(j, lambda cut: wait_recv(cut(src), ri))
            views.append(ld.at[i, :, pl.ds(0, w)])
            copies.append(local(src, views[-1], l_e + i))
            copies[-1].start()
        for cp in copies:
            cp.wait()
        return views

    def from_line(j, d, zp, h=None):
        if h is None:
            return zbs[j].at[d, zp], r_z[j] + d * NZ + zp
        return zbs[j].at[d, zp, h], r_z[j] + (d * NZ + zp) * 2 + h

    def line_event(role, j, e):
        @pl.when(is_role[role])
        def _():
            zp = order(e)
            w = widths[j]
            d = jnp.where(zp > z, 0, 1)
            for h in (0, 1) if j == 0 else (None,):
                o = claim_slot(role)
                dst = outs.at[o, :, pl.ds(0, w)]
                if h is None:
                    srcs = [(gbs[j].at[zp, y], None), (ybs[j].at[zp], r_y[j] + e)]
                    si = s_z[j] + e
                else:
                    srcs = [(gbs[j].at[zp, h], None)]
                    si = s_z[j] + 2 * e + h
                if role == "mid":
                    srcs.append(from_line(j, d, zp, h))
                add_into(dst, fetch(j, srcs))
                z_send(j, dst, e, zp, h)
                slot_last[role][o] = functools.partial(sent_slot, j, o, si)

    def sent_slot(j, o, si):
        per_core(j, lambda cut: wait_send(cut(outs.at[o, :, pl.ds(0, widths[j])]), si))

    def own_shard(role, j, h=None):
        if h is None:
            srcs = [(gbs[j].at[z, y], None), (ybs[j].at[z], r_y[j] + NZ - 1)]
        else:
            srcs = [(gbs[j].at[z, h], None)]
        if role == "mid":
            return srcs + [from_line(j, 0, z, h), from_line(j, 1, z, h)]
        return srcs + [from_line(j, jnp.where(z == 0, 1, 0), z, h)]

    def swap_pieces(j):
        if j == 4:
            return [(None, m * CH, CH, g_conv.at[m], c * CH) for m in range(4)]
        mat = g_ffn.at[{0: 0, 1: 0, 2: 1, 3: 2}[j]]
        w = widths[j]
        if j == 1:
            return [(None, 0, w, mat, c * (FL - FW) + ZF_COLS)]
        return [(0, 0, w, mat, 0), (1, overlap, w - overlap, mat, FL - FW + overlap)]

    swap_sems = [[(take_s(), take_r(), take_l()) for _ in swap_pieces(j)] for j in range(5)]

    def swap(j, o):
        items = []
        for (core, c0, w, mat, to), (si, ri, li) in zip(swap_pieces(j), swap_sems[j]):
            to = to if isinstance(to, int) else pl.multiple_of(to, LANE)
            target = mat.at[:, pl.ds(to, w)]
            mine = outs.at[o, pl.ds(pl.multiple_of(c * DR, DR), DR), pl.ds(c0, w)]
            other = outs.at[o, pl.ds(pl.multiple_of((1 - c) * DR, DR), DR), pl.ds(c0, w)]
            items.append((core, local(mine, target, li), remote(other, target, si, ri, core_dev), target))
        return items

    def swap_start(j, o):
        for core, keep, give, _ in swap(j, o):
            if core is None:
                keep.start()
                give.start()
            else:

                @pl.when(c == core)
                def _():
                    keep.start()
                    give.start()

    def swap_finish(j, o):
        for (core, keep, give, target), (_, ri, _) in zip(swap(j, o), swap_sems[j]):
            if core is None:
                keep.wait()
                give.wait_send()
                wait_recv(target, ri)
            else:

                @pl.when(c == core)
                def _():
                    keep.wait()
                    give.wait_send()

                @pl.when(c != core)
                def _():
                    wait_recv(target, ri)

    def final_event(role, j):
        @pl.when(is_role[role])
        def _():
            o = claim_slot(role)
            w = widths[j]
            add_into(outs.at[o, :, pl.ds(0, w)], fetch(j, own_shard(role, j)))
            swap_start(j, o)
            slot_last[role][o] = functools.partial(swap_finish, j, o)

    s_f0, r_f0 = take_s(), take_r()
    w0 = widths[0]

    def final0_send(role):
        @pl.when(is_role[role])
        def _():
            o = claim_slot(role)
            dst = outs.at[o, :, pl.ds(0, w0)]
            add_into(dst, fetch(0, own_shard(role, 0, 1 - y)))
            cp = local(dst, gb0.at[z, 1 - y], l_e)
            cp.start()
            cp.wait()
            src = gb0.at[z, 1 - y]
            per_core(0, lambda cut: remote(cut(src), cut(yb0), s_f0, r_f0, y_dev).start())

    def final0_finish(role):
        @pl.when(is_role[role])
        def _():
            o = claim_slot(role)
            dst = outs.at[o, :, pl.ds(0, w0)]
            add_into(dst, fetch(0, own_shard(role, 0, y)))
            add_into(dst, [dst] + fetch(0, [(yb0, r_f0)]))
            swap_start(0, o)
            slot_last[role][o] = functools.partial(swap_finish, 0, o)

    def hook(name):
        for role, event in SCHEDULE.get(name, ()):
            if event == "pair":
                final0_send(role)
            elif event == "pair sum":
                final0_finish(role)
            elif event[1] == NZ - 1:
                final_event(role, event[0])
            else:
                line_event(role, *event)

    def chunks(name, count, body):
        first = 0
        for k in range(count):
            if SCHEDULE.get(name + str(k)) or k == count - 1:
                lax.fori_loop(first, k + 1, body, 0)
                first = k + 1
                hook(name + str(k))

    HALF = 2 * ROWS_CHUNK

    def split_sum(name, product, cr, xr, base_d):
        s_c, r_c = take_s(2), take_r(2)
        s_x, r_x = take_s(NCH), take_r(NCH)
        l_c = take_l()

        def give(k, _):
            def tile(n, _):
                cols = pl.ds(pl.multiple_of(n * 512, 512), 512)
                v = product(1, k * HALF, n).astype(BF)
                gall[pl.ds(2 * k, 2), :, cols] = v.reshape(2, ROWS_CHUNK, 512)
                return 0

            lax.fori_loop(0, D // 512, tile, 0)
            remote(
                gall.at[pl.ds(2 * k, 2)], cr.at[pl.ds(2 * k, 2)], s_c + k, r_c + k, core_dev
            ).start()
            return 0

        lax.fori_loop(0, 2, give, 0)
        hook(name + "A")

        def keep(k, _):
            src = cr.at[pl.ds(2 * k, 2)]
            wait_recv(src, r_c + k)
            cp = local(src, rb, l_c)
            cp.start()
            cp.wait()

            def tile(n, _):
                cols = pl.ds(pl.multiple_of(n * 512, 512), 512)
                v = product(0, k * HALF, n) + rb[:, :, cols].reshape(HALF, 512).astype(F32)
                ring[pl.ds(base_d + 2 * k, 2), :, cols] = v.astype(BF).reshape(2, ROWS_CHUNK, 512)
                return 0

            lax.fori_loop(0, D // 512, tile, 0)
            for i in range(2):
                remote(
                    ring.at[base_d + 2 * k + i], xr.at[2 * k + i], s_x + 2 * k + i, r_x + 2 * k + i, x_dev
                ).start()
            return 0

        lax.fori_loop(0, 2, keep, 0)
        for k in range(2):
            wait_send(gall.at[pl.ds(2 * k, 2)], s_c + k)
        hook(name + "D")
        return s_x, r_x

    def rows_at(ref, slot, r0):
        return ref[slot, pl.ds(pl.multiple_of(r0, HALF), HALF), :]

    def dh_product(slot, r0, n):
        cols = pl.ds(pl.multiple_of(n * 512, 512), 512)
        return nt(rows_at(dg, slot, r0), wg_v[cols, :]) + nt(rows_at(du, slot, r0), wu_v[cols, :])

    def dn_product(slot, r0, n):
        cols = pl.ds(pl.multiple_of(n * 512, 512), 512)
        return nn(rows_at(hid, slot, r0), wd_v[:, cols])

    s_xdh, r_xdh = split_sum("dh", dh_product, cr_dh, xr_dh, 0)
    s_xdn, r_xdn = split_sum("dn", dn_product, cr_dn, xr_dn, 4)
    for cp in load_w_in():
        cp.start()
    ld_wout = local(w_out, wd_v.at[pl.ds(0, CL), :], l_wout)
    ld_wout.start()

    s_do, r_do = take_s(NCH), take_r(NCH)

    def ffn_norm_back(k, _):
        rows = pl.ds(pl.multiple_of(k * ROWS_CHUNK, ROWS_CHUNK), ROWS_CHUNK)
        wait_recv(xr_dh.at[k], r_xdh + k)
        d_h = ring[k].astype(F32) + xr_dh[k].astype(F32)
        res = resid[rows, :]
        s2 = inv_rms(res)
        n2 = res * s2
        sm[0, 1:2, :] += jnp.sum(d_h * n2, axis=0, keepdims=True)
        e2 = d_h * gain_ffn_row
        d_res = dy_v[0, rows, :].astype(F32) + s2 * (
            e2 - n2 * jnp.mean(e2 * n2, axis=-1, keepdims=True)
        )
        h2_v[0, rows, :] = d_res.astype(BF)
        remote(h2_v.at[0, rows], h2_v.at[1, rows], s_do + k, r_do + k, core_dev).start()
        return 0

    chunks("nb", NCH, ffn_norm_back)
    for k in range(NCH):
        wait_send(ring.at[k], s_xdh + k)

    for cp in load_w_in():
        cp.wait()
    ld_wout.wait()
    for q in range(S):

        def conv_back(j, _, q=q):
            cols = pl.ds(pl.multiple_of(j * 256, 256), 256)
            rows = pl.ds(q * T, T)
            now, one, two = conv_terms(
                bx[rows, cols].astype(F32), halo_r[q, :, cols].astype(F32), row_iota
            )
            k0, k1, k2 = tap_cols(cols)
            cv = k0 * two + k1 * one + k2 * now
            d_g = nt(h2_v[0, q * T : q * T + T, :], wd_v[cols, :])
            d_cv = d_g * pc[rows, cols].astype(F32)
            sm[0, 2:3, cols] += jnp.sum(d_cv * two, axis=0, keepdims=True)
            sm[0, 3:4, cols] += jnp.sum(d_cv * one, axis=0, keepdims=True)
            sm[0, 4:5, cols] += jnp.sum(d_cv * now, axis=0, keepdims=True)
            after1 = jnp.where(row_iota < T - 1, pltpu.roll(d_cv, T - 1, 0), 0.0)
            after2 = jnp.where(row_iota < T - 2, pltpu.roll(d_cv, T - 2, 0), 0.0)
            d_bx = k2 * d_cv + k1 * after1 + k0 * after2
            dhalo_s[q, :, cols] = d_cv[0:8]
            tail[q, :, cols] = d_bx[T - 16 : T]
            old_b = pb[rows, cols]
            old_x = px[rows, cols]
            pb_tail[q, :, cols] = old_b[T - 16 : T]
            px_tail[q, :, cols] = old_x[T - 16 : T]
            low = d_bx.astype(BF).astype(F32)
            pb[rows, cols] = (low * old_x.astype(F32)).astype(BF)
            px[rows, cols] = (low * old_b.astype(F32)).astype(BF)
            pc[rows, cols] = (d_g * cv).astype(BF)
            return 0

        lax.fori_loop(0, NC, conv_back, 0)

    s_dha, r_dha = take_s(), take_r()
    send_dhalo = remote(dhalo_s, dhalo_r, s_dha, r_dha, prev_dev)

    @pl.when(has_prev)
    def _():
        send_dhalo.start()

    y_send(3, 2)

    hook("cb")

    s_x1, r_x1 = take_s(NCH), take_r(NCH)

    def d1_part(name, ids):
        def tile(n, _):
            cols = pl.ds(pl.multiple_of(n * 512, 512), 512)

            def rows_of(ref):
                return jnp.concatenate(
                    [ref[k * ROWS_CHUNK : (k + 1) * ROWS_CHUNK, :] for k in ids], axis=0
                )

            v = (
                nt(rows_of(pb), wg_v[cols, 0:CL])
                + nt(rows_of(pc), wg_v[cols, CL : 2 * CL])
                + nt(rows_of(px), wu_v[cols, 0:CL])
            ).astype(BF)
            for i, k in enumerate(ids):
                ring[k, :, cols] = v[i * ROWS_CHUNK : (i + 1) * ROWS_CHUNK]
            return 0

        lax.fori_loop(0, D // 512, tile, 0)
        for k in ids:
            remote(ring.at[k], xr_d1.at[k], s_x1 + k, r_x1 + k, x_dev).start()
        hook(name)

    d1_part("d1a", [q * CPS + k for q in range(S) for k in range(CPS - 1)])

    @pl.when(has_next)
    def _():
        wait_recv(dhalo_r, r_dha)

    @pl.when(jnp.logical_not(has_next))
    def _():
        dhalo_r[...] = jnp.zeros_like(dhalo_r)

    tail_iota = lax.broadcasted_iota(jnp.int32, (16, CL), 0)
    for q in range(S):
        first = jnp.broadcast_to(dhalo_r[q, 0:1, :], (16, CL))
        second = jnp.broadcast_to(dhalo_r[q, 1:2, :], (16, CL))
        fix = jnp.where(
            tail_iota == 14,
            k_taps[0] * first,
            jnp.where(tail_iota == 15, k_taps[1] * first + k_taps[0] * second, 0.0),
        )
        low = (tail[q] + fix).astype(BF).astype(F32)
        rows = pl.ds(q * T + T - 16, 16)
        pb[rows, :] = (low * px_tail[q].astype(F32)).astype(BF)
        px[rows, :] = (low * pb_tail[q].astype(F32)).astype(BF)

    s_dp, r_dp = take_s(4), take_r(4)
    theirs = pl.ds(pl.multiple_of((1 - c) * CH, LANE), CH)
    ours = pl.ds(pl.multiple_of(c * CH, LANE), CH)
    dp_sends = [
        remote(ref.at[:, theirs], dy_v.at[1, :, pl.ds(m * CH, CH)], s_dp + m, r_dp + m, core_dev)
        for m, ref in enumerate((pb, pc, px, gated))
    ]
    for cp in dp_sends:
        cp.start()
    hook("tail")

    d1_part("d1b", [q * CPS + k for q in range(S) for k in range(1, CPS)])

    for q in range(S):
        wait_recv(h1_v.at[1, pl.ds(q * T, T)], r_h1 + q)
    for k in range(NCH):
        rows = pl.ds(k * ROWS_CHUNK, ROWS_CHUNK)
        wait_recv(h2_v.at[1, rows], r_do + k)
    for m in range(4):
        wait_recv(dy_v.at[1, :, pl.ds(m * CH, CH)], r_dp + m)
    W4 = widths[4]
    g4 = [dg.at[i, pl.ds(k * SR, SR), pl.ds(0, W4)] for i in range(2) for k in range(2)]

    def g_mixer(u, _):
        zp = order_dyn(u)
        zc = pl.ds(pl.multiple_of(zp * GR, GR), GR)
        for m, (mine, lhs) in enumerate(((pb, h1_v), (pc, h1_v), (px, h1_v), (gated, h2_v))):
            v = tn(lhs[0, :, zc], mine[:, ours]) + tn(
                lhs[1, :, zc], dy_v[1, :, m * CH : (m + 1) * CH]
            )
            v = v.astype(BF)
            g4[0][:, m * CH : (m + 1) * CH] = v[:SR]
            g4[1][:, m * CH : (m + 1) * CH] = v[SR:]
        cps = [local(g4[h], gb4.at[zp, h], l_g + h) for h in range(2)]
        for cp in cps:
            cp.start()
        for cp in cps:
            cp.wait()

        @pl.when(u < NZ - 1)
        def _():
            y_send(4, u)

        return 0

    chunks("gc", NZ, g_mixer)
    for j in (1, 2, 3, 4):
        y_send(j, NZ - 1)

    l_o = take_l(2)

    def put_rows(v, out, rows, n):
        slot = n % 2
        cp = local(rb.at[slot], out.at[rows, :], l_o + slot)

        @pl.when(n >= 2)
        def _():
            cp.wait()

        rb[slot] = v
        cp.start()

    def put_done(out):
        for slot in range(2):
            local(rb.at[slot], out.at[pl.ds(0, ROWS_CHUNK), :], l_o + slot).wait()

    def block_chunk(k, _):
        rows = pl.ds(pl.multiple_of(k * ROWS_CHUNK, ROWS_CHUNK), ROWS_CHUNK)
        wait_recv(xr_dn.at[k], r_xdn + k)
        total = ring[4 + k].astype(F32) + xr_dn[k].astype(F32)
        put_rows((resid[rows, :] + total).astype(BF), block_out, rows, k)
        return 0

    chunks("blk", NCH, block_chunk)
    put_done(block_out)

    def mix_norm_back(n, _):
        k = (n % S) * CPS + n // S
        rows = pl.ds(pl.multiple_of(k * ROWS_CHUNK, ROWS_CHUNK), ROWS_CHUNK)
        wait_recv(xr_d1.at[k], r_x1 + k)
        d_h = ring[k].astype(F32) + xr_d1[k].astype(F32)
        xv = tok_v[rows, :].astype(F32)
        s1 = inv_rms(xv)
        n1 = xv * s1
        sm[0, 0:1, :] += jnp.sum(d_h * n1, axis=0, keepdims=True)
        e1 = d_h * gain_mix_row
        out = h2_v[0, rows, :].astype(F32) + s1 * (
            e1 - n1 * jnp.mean(e1 * n1, axis=-1, keepdims=True)
        )
        put_rows(out.astype(BF), d_tokens, rows, n)
        return 0

    chunks("dt", NCH, mix_norm_back)
    put_done(d_tokens)

    s_sm, r_sm = take_s(2 * NZ), take_r(2 * NZ)
    a = remote(sm.at[0], sm_r.at[0], s_sm, r_sm, core_dev)
    a.start()
    a.wait()
    sm[1] = sm[0] + sm_r[0]
    for k, dev in others:
        remote(sm.at[1], sm_r.at[k], s_sm + k, r_sm + k, dev).start()
    hook("sm")

    total = sm[1]
    for k, _ in others:
        wait_recv(sm_r.at[k], r_sm + k)
        total = total + sm_r[k]
    for k, _ in others:
        wait_send(sm.at[1], s_sm + k)
    sm[0] = total
    out_small = local(sm.at[0], small_out, l_small)
    out_small.start()
    out_small.wait()

    for role, cond in is_role.items():

        @pl.when(cond)
        def _(role=role):
            for finish in slot_last[role]:
                if finish is not None:
                    finish()

    @pl.when(end)
    def _():
        for e in range(NZ - 1):
            for h in range(2):
                per_core(0, lambda cut: wait_send(cut(gb0.at[0, h]), s_z[0] + 2 * e + h))

    for j in range(1, 5):
        for u in range(NZ):
            per_core(j, lambda cut: wait_send(cut(ybs[j].at[0]), s_y[j] + u))
    per_core(0, lambda cut: wait_send(cut(yb0), s_f0))
    for q in range(S):
        h1_send(q).wait_send()
    for k in range(NCH):
        wait_send(h2_v.at[0, pl.ds(k * ROWS_CHUNK, ROWS_CHUNK)], s_do + k)
        wait_send(ring.at[k], s_x1 + k)
        wait_send(ring.at[4 + k], s_xdn + k)
    for cp in dp_sends:
        cp.wait_send()

    @pl.when(has_next)
    def _():
        for q in range(S):
            halo_send(q).wait_send()

    @pl.when(has_prev)
    def _():
        send_dhalo.wait_send()


def fused_body(tokens, gain_mix, w_in, kernel, w_out, gain_ffn, w_gate, w_up, w_down, cotangent):
    S, T, D = tokens.shape
    CL = w_out.shape[0]
    FL = w_gate.shape[1]
    R = S * T
    n_seq = lax.axis_size("seq")
    tiles = FL // LANE
    FW = -(-tiles // 2) * LANE
    GR = D // NZ
    SR = GR // 2
    DR = SR // 2
    widths = [ZF_COLS, FW - ZF_COLS, FW, FW, 2 * CL]
    NCH = R // ROWS_CHUNK

    def sds(shape, dtype=BF):
        return jax.ShapeDtypeStruct(shape, dtype)

    outs = [sds((R, D)), sds((R, D)), sds((3, DR, FL)), sds((4, DR, CL)), sds((8, D), F32)]
    outs += [sds((NZ, 2, SR, w)) for w in widths]
    outs += [sds((SR, widths[0]))] + [sds((NZ, SR, w)) for w in widths[1:]]
    outs += [sds((2, NZ, 2, SR, widths[0]))] + [sds((2, NZ, SR, w)) for w in widths[1:]]
    outs += [sds((NCH, ROWS_CHUNK, D))] * 2
    any_spec = pl.BlockSpec(memory_space=pl.ANY)
    V = pltpu.VMEM
    scratch = [
        V((D,), F32),
        V((3, CL), F32),
        V((D,), F32),
        V((R, D), BF),
        V((D, FW), BF),
        V((D, FW), BF),
        V((FW, D), BF),
        V((2, R, D), BF),
        V((2, R, D), BF),
        V((2, R, D), BF),
        V((2, R, FW), BF),
        V((2, R, FW), BF),
        V((2, R, FW), BF),
        V((R, CL), BF),
        V((R, CL), BF),
        V((R, CL), BF),
        V((R, CL), BF),
        V((R, CL), BF),
        V((R, D), F32),
        V((NCH, ROWS_CHUNK, D), BF),
        V((8, ROWS_CHUNK, D), BF),
        V((NCH, ROWS_CHUNK, D), BF),
        V((NCH, ROWS_CHUNK, D), BF),
        V((NCH, ROWS_CHUNK, D), BF),
        V((2, ROWS_CHUNK, D), BF),
        V((4, SR, FW), BF),
        V((4, SR, FW), BF),
        V((S, 16, CL), BF),
        V((S, 16, CL), BF),
        V((S, 8, CL), F32),
        V((S, 8, CL), F32),
        V((S, 16, CL), F32),
        V((S, 16, CL), BF),
        V((S, 16, CL), BF),
        V((2, 8, D), F32),
        V((2 * NZ, 8, D), F32),
        pltpu.SemaphoreType.DMA((N_SEND,)),
        pltpu.SemaphoreType.DMA((N_RECV,)),
        pltpu.SemaphoreType.DMA((N_LOCAL,)),
    ]
    flops = 2 * R * D * (4 * CL + 3 * FL) * 3
    res = pl.pallas_call(
        functools.partial(step_kernel, (R, T, D, CL, FL, FW)),
        out_shape=outs,
        in_specs=[any_spec] * 10,
        out_specs=[any_spec] * len(outs),
        scratch_shapes=scratch,
        compiler_params=pltpu.CompilerParams(
            collective_id=0, has_side_effects=True, vmem_limit_bytes=63 << 20
        ),
        cost_estimate=pl.CostEstimate(flops=flops, bytes_accessed=200 << 20, transcendentals=0),
        name="block_step",
    )(
        tokens.reshape(R, D), gain_mix, w_in, kernel, w_out,
        gain_ffn, w_gate, w_up, w_down, cotangent.reshape(R, D),
    )
    block_out, d_tokens, g_mix, g_in, g_taps, g_out, g_gain, g_gate, g_up, g_down = finish(
        n_seq, *res[:5]
    )
    return (
        block_out.reshape(S, T, D),
        d_tokens.reshape(S, T, D),
        g_mix, g_in, g_taps, g_out.T, g_gain, g_gate, g_up, g_down.T,
    )


def finish_kernel(
    n_seq, block_in, d_in, ffn_in, conv_in, small_in,
    block_out, d_out, g_mix, g_in, g_taps, g_out, g_gain, g_gate, g_up, g_down,
    block_v, d_v, ffn, conv, small, gate_v, up_v, down_v, in_v, out_v, mix_v, taps_v, gain_v, sem,
):
    D = d_in.shape[1]
    CL = conv_in.shape[2]
    s = lax.axis_index("seq")
    count = [0]

    def copy(src, dst):
        count[0] += 1
        cp = pltpu.make_async_copy(src, dst, sem.at[count[0] - 1])
        cp.start()
        return cp

    loads = [copy(ffn_in.at[0], ffn.at[0]), copy(conv_in, conv), copy(small_in, small)]
    loads += [copy(ffn_in.at[m], ffn.at[m]) for m in (1, 2)]
    passing = [copy(block_in, block_v), copy(d_in, d_v)]
    stores = []
    loads[0].wait()
    down_v[...] = ffn[0].astype(F32)
    stores.append(copy(down_v, g_down))
    loads[1].wait()
    in_v[...] = conv[0:3].astype(F32)
    stores.append(copy(in_v, g_in))
    out_v[...] = conv[3].astype(F32)
    stores.append(copy(out_v, g_out))
    passing[0].wait()
    stores.append(copy(block_v, block_out))
    passing[1].wait()
    stores.append(copy(d_v, d_out))
    loads[3].wait()
    gate_v[...] = ffn[1].astype(F32)
    stores.append(copy(gate_v, g_gate))
    loads[4].wait()
    up_v[...] = ffn[2].astype(F32)
    stores.append(copy(up_v, g_up))
    loads[2].wait()
    per_d, per_c = D // n_seq, CL // n_seq
    mine = pltpu.roll(small[...], D - s * per_d, 1)
    mix_v[...] = mine[0, 0:per_d]
    gain_v[...] = mine[1, 0:per_d]
    mine = pltpu.roll(small[...], D - s * per_c, 1)
    for t in range(3):
        taps_v[t] = mine[2 + t : 3 + t, 0:per_c]
    stores += [copy(mix_v, g_mix), copy(gain_v, g_gain), copy(taps_v, g_taps)]
    for cp in stores:
        cp.wait()


def finish(n_seq, block_out, d_tokens, g_ffn, g_conv, small):
    R, D = block_out.shape
    _, DR, FL = g_ffn.shape
    CL = g_conv.shape[2]
    any_spec = pl.BlockSpec(memory_space=pl.ANY)
    V = pltpu.VMEM
    tails = [
        (DR, FL), (DR, FL), (DR, FL), (3, DR, CL), (DR, CL),
        (D // n_seq,), (3, 1, CL // n_seq), (D // n_seq,),
    ]
    gate, up, down, inp, out, mix, taps, gain = [jax.ShapeDtypeStruct(t, F32) for t in tails]
    low = jax.ShapeDtypeStruct((R, D), BF)
    return pl.pallas_call(
        functools.partial(finish_kernel, n_seq),
        out_shape=[low, low, mix, inp, taps, out, gain, gate, up, down],
        in_specs=[any_spec] * 5,
        out_specs=[any_spec] * 10,
        scratch_shapes=[V((R, D), BF), V((R, D), BF), V(g_ffn.shape, BF), V(g_conv.shape, BF), V(small.shape, F32)]
        + [V(t, F32) for t in tails]
        + [pltpu.SemaphoreType.DMA((20,))],
        compiler_params=pltpu.CompilerParams(vmem_limit_bytes=63 << 20),
        name="finish",
    )(block_out, d_tokens, g_ffn, g_conv, small)


def from_behind(value, axis, by):
    count = lax.axis_size(axis)
    pairs = [(i, i + by) for i in range(count) if 0 <= i + by < count]
    return lax.ppermute(value, axis, pairs)


def rms_scale(vector):
    return lax.rsqrt(jnp.mean(vector * vector, axis=-1, keepdims=True) + epsilon)


def norm_back(d_normout, normed, inv_scale, gain_vec):
    d_normed = d_normout * gain_vec
    return inv_scale * (d_normed - normed * jnp.mean(d_normed * normed, axis=-1, keepdims=True))


def matmul(lhs_mat, rhs_mat):
    return jnp.dot(lhs_mat, rhs_mat, preferred_element_type=jnp.float32)


def left_trans(lhs_mat, rhs_mat):
    return lax.dot_general(
        lhs_mat, rhs_mat, (((0,), (0,)), ((), ())), preferred_element_type=jnp.float32
    )


def right_trans(lhs_mat, rhs_mat):
    return lax.dot_general(
        lhs_mat, rhs_mat, (((1,), (1,)), ((), ())), preferred_element_type=jnp.float32
    )


def general_body(tokens, gain_mix, w_in, kernel, w_out, gain_ffn, w_gate, w_up, w_down, cotangent):
    seq_count, tok_rows, model_width = tokens.shape
    row_count = seq_count * tok_rows
    tokens_f = tokens.astype(jnp.float32).reshape(row_count, model_width)
    scale_mix = rms_scale(tokens_f)
    normed_mix = tokens_f * scale_mix
    h_mix = (normed_mix * gain_mix).astype(jnp.bfloat16)
    proj_b = matmul(h_mix, w_in[0])
    proj_c = matmul(h_mix, w_in[1])
    proj_x = matmul(h_mix, w_in[2])
    conv_in = (proj_b * proj_x).astype(jnp.bfloat16).reshape(seq_count, tok_rows, -1)
    before = from_behind(conv_in[:, tok_rows - 2 :, :], "seq", 1)
    extended = jnp.concatenate([before, conv_in], axis=1).astype(jnp.float32)
    conv_out = (
        kernel[0] * extended[:, :-2] + kernel[1] * extended[:, 1:-1] + kernel[2] * extended[:, 2:]
    )
    conv_flat = conv_out.reshape(row_count, -1)
    gated = (proj_c * conv_flat).astype(jnp.bfloat16)
    mixed_sum = lax.psum(matmul(gated, w_out).astype(jnp.bfloat16), "chan").astype(jnp.float32)
    residual = tokens_f + mixed_sum
    scale_ffn = rms_scale(residual)
    normed_ffn = residual * scale_ffn
    h_ffn = (normed_ffn * gain_ffn).astype(jnp.bfloat16)
    gate_pre = matmul(h_ffn, w_gate)
    up_value = matmul(h_ffn, w_up)
    sigmoid_gate = jax.nn.sigmoid(gate_pre)
    silu_gate = gate_pre * sigmoid_gate
    hidden = (silu_gate * up_value).astype(jnp.bfloat16)
    ffn_total = lax.psum(matmul(hidden, w_down).astype(jnp.bfloat16), "chan").astype(jnp.float32)
    block_out = (
        (residual + ffn_total).astype(jnp.bfloat16).reshape(seq_count, tok_rows, model_width)
    )
    grad_out = cotangent.reshape(row_count, model_width)
    g_w_down = left_trans(hidden, grad_out)
    d_hidden = right_trans(grad_out, w_down)
    d_gate = (d_hidden * up_value * sigmoid_gate * (1.0 + gate_pre * (1.0 - sigmoid_gate))).astype(
        jnp.bfloat16
    )
    d_up = (d_hidden * silu_gate).astype(jnp.bfloat16)
    g_w_gate = left_trans(h_ffn, d_gate)
    g_w_up = left_trans(h_ffn, d_up)
    d_h_ffn = lax.psum(
        (right_trans(d_gate, w_gate) + right_trans(d_up, w_up)).astype(jnp.bfloat16), "chan"
    ).astype(jnp.float32)
    g_gain_ffn = jnp.sum(d_h_ffn * normed_ffn, axis=0)
    d_resid = grad_out.astype(jnp.float32) + norm_back(d_h_ffn, normed_ffn, scale_ffn, gain_ffn)
    d_mixed = d_resid.astype(jnp.bfloat16)
    g_w_out = left_trans(gated, d_mixed)
    d_gated = right_trans(d_mixed, w_out)
    d_proj_c = (d_gated * conv_flat).astype(jnp.bfloat16)
    d_conv = (d_gated * proj_c).reshape(seq_count, tok_rows, -1)
    after_rows = from_behind(d_conv[:, :2, :], "seq", -1)
    ext_back = jnp.concatenate([d_conv, after_rows], axis=1)
    d_conv_in = (
        kernel[2] * ext_back[:, :-2] + kernel[1] * ext_back[:, 1:-1] + kernel[0] * ext_back[:, 2:]
    )
    g_kernel = jnp.stack(
        [
            jnp.sum(d_conv * extended[:, :-2], axis=(0, 1)),
            jnp.sum(d_conv * extended[:, 1:-1], axis=(0, 1)),
            jnp.sum(d_conv * extended[:, 2:], axis=(0, 1)),
        ]
    ).reshape(3, 1, -1)
    d_conv_low = d_conv_in.reshape(row_count, -1).astype(jnp.bfloat16)
    d_proj_b = (d_conv_low * proj_x).astype(jnp.bfloat16)
    d_proj_x = (d_conv_low * proj_b).astype(jnp.bfloat16)
    g_w_in = jnp.stack(
        [left_trans(h_mix, d_proj_b), left_trans(h_mix, d_proj_c), left_trans(h_mix, d_proj_x)]
    )
    d_h_mix = lax.psum(
        (
            right_trans(d_proj_b, w_in[0])
            + right_trans(d_proj_c, w_in[1])
            + right_trans(d_proj_x, w_in[2])
        ).astype(jnp.bfloat16),
        "chan",
    ).astype(jnp.float32)
    g_gain_mix = jnp.sum(d_h_mix * normed_mix, axis=0)
    d_tokens = (
        (d_resid + norm_back(d_h_mix, normed_mix, scale_mix, gain_mix))
        .astype(jnp.bfloat16)
        .reshape(seq_count, tok_rows, model_width)
    )
    summed = (
        lax.psum_scatter(g_w_in, "seq", scatter_dimension=1, tiled=True),
        lax.psum_scatter(g_w_out, "seq", scatter_dimension=1, tiled=True),
        lax.psum_scatter(g_kernel, "seq", scatter_dimension=2, tiled=True),
        lax.psum_scatter(g_gain_mix, "seq", scatter_dimension=0, tiled=True),
        lax.psum_scatter(g_w_gate, "seq", scatter_dimension=0, tiled=True),
        lax.psum_scatter(g_w_up, "seq", scatter_dimension=0, tiled=True),
        lax.psum_scatter(g_w_down, "seq", scatter_dimension=1, tiled=True),
        lax.psum_scatter(g_gain_ffn, "seq", scatter_dimension=0, tiled=True),
    )
    sum_in, sum_out, sum_kernel, sum_gain_mix, sum_gate, sum_up, sum_down, sum_gain_ffn = summed
    return (
        block_out,
        d_tokens,
        sum_gain_mix,
        sum_in,
        sum_kernel,
        sum_out,
        sum_gain_ffn,
        sum_gate,
        sum_up,
        sum_down,
    )


def solution(mesh):
    body = fused_body if mesh.shape["seq"] == 4 * NZ else general_body
    placed = (
        P(None, "seq", None),
        P(),
        P(None, None, "chan"),
        P(None, "chan"),
        P("chan", None),
        P(),
        P(None, "chan"),
        P(None, "chan"),
        P("chan", None),
        P(None, "seq", None),
    )
    return jax.shard_map(
        body,
        mesh=mesh,
        in_specs=placed,
        out_specs=(
            P(None, "seq", None),
            P(None, "seq", None),
            P("seq"),
            P(None, "seq", "chan"),
            P(None, "chan", "seq"),
            P("chan", "seq"),
            P("seq"),
            P("seq", "chan"),
            P("seq", "chan"),
            P("chan", "seq"),
        ),
        check_vma=False,
    )
```

profile of v0, /device:TPU:0, one launch (start us, length us, event | category | flops | bytes accessed | tf_op | source)
XLA Modules:
  0.0 263.3 jit_solution(596044192637217845)
XLA Ops:
  0.6 256.3 %block_step.1 = (bf16[512,1536]{1,0:T(8,128)(2,1)}, bf16[512,1536]{1,0:T(8,128)(2,1)}, bf16[3,96,3456]{2,1,0:T(8,128)(2,1)}, bf16[4,96,768]{2,1,0:T(8,128)(2,1)}...) custom-call(bf16[512,1536]{1,0:T(8,128)(2,1)} %bitcast.6, ...), custom_call_target="tpu_custom_call" | custom-call | flops 63417876480 | bytes 209715200 | tf_op jit(solution)/shard_map/block_step/pallas_call | solution.py:1133
  256.9 6.2 %finish.1 = (bf16[512,1536]{1,0:T(8,128)(2,1)}, bf16[512,1536]{1,0:T(8,128)(2,1)}, f32[96]{0:T(128)}, f32[3,96,768]{2,1,0:T(8,128)}, f32[3,1,48]{2,1,0:T(1,128)}...) custom-call(bf16[512,1536]{1,0:T(8,128)(2,1)} %get-tuple-element.25.block_, ...), custom_call_target="tpu_custom_call" | custom-call | tf_op jit(solution)/shard_map/finish/pallas_call | solution.py:1221
where the time goes:
time: 265 us; the launch traced here: 263 us
  Pallas kernels  262 us (99%)
    pallas_call x1, Pallas kernels, fused_body(): pl.pallas_call(functools.partial(step_kernel, (R, T, D, CL, FL, FW)), out...  256 us
    pallas_call x1, Pallas kernels, finish(): pl.pallas_call(functools.partial(finish_kernel, n_seq), out_shape=[low, l...  6.22 us

commit v1 on v0

--- a/solution.py
+++ b/solution.py
@@ -14,6 +14,7 @@
 LANE = 128
 NZ = 4
 ROWS_CHUNK = 128
+SMALL = 256
 ZF_COLS = 1152
 
 
@@ -72,7 +73,7 @@
     cr_dh, cr_dn,
     gain_mix, taps, gain_ffn, tok_v, wg_v, wu_v, wd_v, dy_v, h2_v, h1_v, hid, dg, du, pb, pc, px, bx, gated, resid, gall,
     ring, xr_dh, xr_dn, xr_d1, rb, ld, outs, halo_s, halo_r, dhalo_s, dhalo_r, tail, pb_tail, px_tail,
-    sm, sm_r, ss, rs, ls,
+    sm, sm_o, sm_t, sm_r, ss, rs, ls,
 ):
     R, T, D, CL, FL, FW = dims
     S = R // T
@@ -153,40 +154,56 @@
     greet(next_dev)
     pl.semaphore_wait(bar, 3 + 2 * NZ)
 
-    QR, SUBS = CL // 4, 4
-    PR = QR // SUBS
-    s_w, r_w = [take_s(SUBS) for _ in range(4)], [take_r(SUBS) for _ in range(4)]
-
-    def w_rows(half, quarter, sub):
-        return wd_v.at[pl.ds(pl.multiple_of(half * CL + quarter * QR + sub * PR, PR), PR), :]
-
-    mine_q, pair_q = y * 2 + c, (1 - y) * 2 + c
-    core_q, far_q = y * 2 + (1 - c), (1 - y) * 2 + (1 - c)
+    SUBS = 2
+    ER = CL // 8
+    PR = ER // SUBS
+    zi = z % 2
+    z_dev = did(z + 1 - 2 * zi, y, c)
+    mine_e = zi * 4 + y * 2 + c
+    pair_e = zi * 4 + (1 - y) * 2 + c
+    line_e = (1 - zi) * 4 + y * 2 + c
+    far_e = (1 - zi) * 4 + (1 - y) * 2 + c
+    w_sems = {}
+
+    def w_rows(half, eighth, sub):
+        return wd_v.at[pl.ds(pl.multiple_of(half * CL + eighth * ER + sub * PR, PR), PR), :]
+
+    def w_copy(name, eighth, sub, dev):
+        if (name, sub) not in w_sems:
+            w_sems[name, sub] = take_s(), take_r()
+        ref = w_rows(1 - x, eighth, sub)
+        return remote(ref, ref, *w_sems[name, sub], dev)
+
+    def w_came(name, eighth, sub):
+        wait_recv(w_rows(1 - x, eighth, sub), w_sems[name, sub][1])
 
     def w_over_x(sub):
-        src = w_out.at[pl.ds(pl.multiple_of(mine_q * QR + sub * PR, PR), PR), :]
-        return remote(src, w_rows(x, mine_q, sub), s_w[0] + sub, r_w[0] + sub, x_dev)
-
-    def w_over_y(sub):
-        ref = w_rows(1 - x, mine_q, sub)
-        return remote(ref, ref, s_w[1] + sub, r_w[1] + sub, y_dev)
-
-    def w_over_core(sub):
-        ref = w_rows(1 - x, mine_q, sub)
-        return remote(ref, ref, s_w[2] + sub, r_w[2] + sub, core_dev)
-
-    def w_far_over_core(sub):
-        ref = w_rows(1 - x, pair_q, sub)
-        return remote(ref, ref, s_w[3] + sub, r_w[3] + sub, core_dev)
-
-    def w_pass_on(sub):
-        wait_recv(w_rows(1 - x, mine_q, sub), r_w[0] + sub)
-        w_over_y(sub).start()
-        w_over_core(sub).start()
-
-    def w_pass_far(sub):
-        wait_recv(w_rows(1 - x, pair_q, sub), r_w[1] + sub)
-        w_far_over_core(sub).start()
+        if ("x", sub) not in w_sems:
+            w_sems["x", sub] = take_s(), take_r()
+        src = w_out.at[pl.ds(pl.multiple_of(mine_e * ER + sub * PR, PR), PR), :]
+        return remote(src, w_rows(x, mine_e, sub), *w_sems["x", sub], x_dev)
+
+    w_sent = []
+
+    def w_pass(name, eighth, sub, targets):
+        w_came(name, eighth, sub)
+        for to, dev in targets:
+            w_copy(to, eighth, sub, dev).start()
+            w_sent.append((to, eighth, sub, dev))
+
+    def w_mine(sub):
+        w_pass("x", mine_e, sub, (("z", z_dev), ("y", y_dev), ("core", core_dev)))
+
+    def w_pair(sub):
+        to = (("zy", z_dev),) if sub == 0 else ()
+        w_pass("y", pair_e, sub, to + (("core pair", core_dev),))
+
+    def w_line(sub):
+        to = (("zy", y_dev),) if sub == 1 else ()
+        w_pass("z", line_e, sub, to + (("core line", core_dev),))
+
+    def w_far(sub):
+        w_pass("zy", far_e, sub, (("core far", core_dev),))
 
     for sub in range(SUBS):
         w_over_x(sub).start()
@@ -257,8 +274,6 @@
             return 0
 
         lax.fori_loop(0, CPS, norm_rows, 0)
-        if q > 0:
-            w_pass_on(1)
         if q == 0:
             for cp in load_w_in():
                 cp.wait()
@@ -292,11 +307,8 @@
 
         for k in range(CPS - 1, 0, -1):
             mixer_out(q * CPS + k)
-        if q == 0:
-            w_pass_on(0)
-        else:
-            w_pass_on(2)
-            w_pass_far(0)
+        if q > 0:
+            w_mine(1)
 
         @pl.when(has_prev)
         def _(q=q):
@@ -316,14 +328,18 @@
 
         lax.fori_loop(0, NC, conv_top, 0)
         mixer_out(q * CPS)
+        if q == 0:
+            w_mine(0)
         h1_send(q).start()
         if q == 0:
             ld_dy.start()
             s_dy, r_dy = take_s(), take_r()
             send_dy = remote(cot, dy_v.at[1], s_dy, r_dy, core_dev)
             send_dy.start()
-    w_pass_on(3)
-    w_pass_far(1)
+    w_line(0)
+    w_pair(0)
+    w_line(1)
+    w_pair(1)
 
     s_h2, r_h2 = take_s(NCH), take_r(NCH)
     ld_wg.wait()
@@ -370,12 +386,12 @@
 
         lax.fori_loop(0, NF, tile, 0, unroll=True)
 
-    w_pass_far(2)
-    w_pass_far(3)
+    for sub in range(SUBS):
+        w_far(sub)
     ld_wout.wait()
     for sub in range(SUBS):
-        wait_recv(w_rows(1 - x, core_q, sub), r_w[2] + sub)
-        wait_recv(w_rows(1 - x, far_q, sub), r_w[3] + sub)
+        for name, eighth in (("core", mine_e), ("core pair", pair_e), ("core line", line_e), ("core far", far_e)):
+            w_came(name, eighth + 1 - 2 * c, sub)
     residual_chunk(sent(0))
 
     def chunk_loop(n, _):
@@ -389,8 +405,8 @@
     lax.fori_loop(0, NCH, chunk_loop, 0)
     for sub in range(SUBS):
         w_over_x(sub).wait_send()
-        for send in (w_over_y, w_over_core, w_far_over_core):
-            send(sub).wait_send()
+    for item in w_sent:
+        w_copy(*item).wait_send()
     ld_wd.start()
     ld_dy.wait()
     send_dy.wait()
@@ -1008,22 +1024,28 @@
     put_done(d_tokens)
 
     s_sm, r_sm = take_s(2 * NZ), take_r(2 * NZ)
-    a = remote(sm.at[0], sm_r.at[0], s_sm, r_sm, core_dev)
+    a = remote(sm.at[0], sm_o, s_sm, r_sm, core_dev)
     a.start()
     a.wait()
-    sm[1] = sm[0] + sm_r[0]
+    chip_sum = sm[0] + sm_o[...]
+    gain_w, tap_w = 2 * D // n_seq, 2 * CL // n_seq
+    is_gain = lax.broadcasted_iota(jnp.int32, sm_t.shape[1:], 0) < 2
+    for q in range(2 * NZ):
+        gains = pltpu.roll(chip_sum, (D - q * gain_w) % D, 1)[:, 0:SMALL]
+        tap_sums = pltpu.roll(chip_sum, (D - q * tap_w) % D, 1)[:, 0:SMALL]
+        sm_t[q] = jnp.where(is_gain, gains, tap_sums)
     for k, dev in others:
-        remote(sm.at[1], sm_r.at[k], s_sm + k, r_sm + k, dev).start()
+        remote(sm_t.at[dev[0] // 2], sm_r.at[k], s_sm + k, r_sm + k, dev).start()
     hook("sm")
 
-    total = sm[1]
+    total = sm_t[s // 2]
     for k, _ in others:
         wait_recv(sm_r.at[k], r_sm + k)
         total = total + sm_r[k]
     for k, _ in others:
-        wait_send(sm.at[1], s_sm + k)
-    sm[0] = total
-    out_small = local(sm.at[0], small_out, l_small)
+        wait_send(sm_t.at[0], s_sm + k)
+    sm_r[0] = total
+    out_small = local(sm_r.at[0], small_out, l_small)
     out_small.start()
     out_small.wait()
 
@@ -1081,7 +1103,7 @@
     def sds(shape, dtype=BF):
         return jax.ShapeDtypeStruct(shape, dtype)
 
-    outs = [sds((R, D)), sds((R, D)), sds((3, DR, FL)), sds((4, DR, CL)), sds((8, D), F32)]
+    outs = [sds((R, D)), sds((R, D)), sds((3, DR, FL)), sds((4, DR, CL)), sds((8, SMALL), F32)]
     outs += [sds((NZ, 2, SR, w)) for w in widths]
     outs += [sds((SR, widths[0]))] + [sds((NZ, SR, w)) for w in widths[1:]]
     outs += [sds((2, NZ, 2, SR, widths[0]))] + [sds((2, NZ, SR, w)) for w in widths[1:]]
@@ -1123,8 +1145,10 @@
         V((S, 16, CL), F32),
         V((S, 16, CL), BF),
         V((S, 16, CL), BF),
-        V((2, 8, D), F32),
-        V((2 * NZ, 8, D), F32),
+        V((1, 8, D), F32),
+        V((8, D), F32),
+        V((2 * NZ, 8, SMALL), F32),
+        V((2 * NZ, 8, SMALL), F32),
         pltpu.SemaphoreType.DMA((N_SEND,)),
         pltpu.SemaphoreType.DMA((N_RECV,)),
         pltpu.SemaphoreType.DMA((N_LOCAL,)),
@@ -1195,10 +1219,10 @@
     stores.append(copy(up_v, g_up))
     loads[2].wait()
     per_d, per_c = D // n_seq, CL // n_seq
-    mine = pltpu.roll(small[...], D - s * per_d, 1)
+    mine = pltpu.roll(small[...], SMALL - (s % 2) * per_d, 1)
     mix_v[...] = mine[0, 0:per_d]
     gain_v[...] = mine[1, 0:per_d]
-    mine = pltpu.roll(small[...], D - s * per_c, 1)
+    mine = pltpu.roll(small[...], SMALL - (s % 2) * per_c, 1)
     for t in range(3):
         taps_v[t] = mine[2 + t : 3 + t, 0:per_c]
     stores += [copy(mix_v, g_mix), copy(gain_v, g_gain), copy(taps_v, g_taps)]

time: 265 us -> 258 us (0.974)
  Pallas kernels: 262 us -> 256 us
    pallas_call x1, Pallas kernels: 256 us -> 250 us  [fused_body(): pl.pallas_call(functools.partial(step_kernel, (R, T, D, CL, FL, FW)), out...]
where the time goes in v1:
time: 258 us; the launch traced here: 257 us
  Pallas kernels  256 us (99%)
    pallas_call x1, Pallas kernels, fused_body(): pl.pallas_call(functools.partial(step_kernel, (R, T, D, CL, FL, FW)), out...  250 us
    pallas_call x1, Pallas kernels, finish(): pl.pallas_call(functools.partial(finish_kernel, n_seq), out_shape=[low, l...  6.22 us

profile of v1, /device:TPU:0, one launch (start us, length us, event | category | flops | bytes accessed | tf_op | source)
XLA Modules:
  0.0 256.6 jit_solution(10856788524397957724)
XLA Ops:
  0.6 249.5 %block_step.1 = (bf16[512,1536]{1,0:T(8,128)(2,1)}, bf16[512,1536]{1,0:T(8,128)(2,1)}, bf16[3,96,3456]{2,1,0:T(8,128)(2,1)}, bf16[4,96,768]{2,1,0:T(8,128)(2,1)}...) custom-call(bf16[512,1536]{1,0:T(8,128)(2,1)} %bitcast.6, ...), custom_call_target="tpu_custom_call" | custom-call | flops 63417876480 | bytes 209715200 | tf_op jit(solution)/shard_map/block_step/pallas_call | solution.py:1157
  250.2 6.2 %finish.1 = (bf16[512,1536]{1,0:T(8,128)(2,1)}, bf16[512,1536]{1,0:T(8,128)(2,1)}, f32[96]{0:T(128)}, f32[3,96,768]{2,1,0:T(8,128)}, f32[3,1,48]{2,1,0:T(1,128)}...) custom-call(bf16[512,1536]{1,0:T(8,128)(2,1)} %get-tuple-element.25.block_, ...), custom_call_target="tpu_custom_call" | custom-call | tf_op jit(solution)/shard_map/finish/pallas_call | solution.py:1245

commit v2 on v1

--- a/solution.py
+++ b/solution.py
@@ -15,7 +15,7 @@
 NZ = 4
 ROWS_CHUNK = 128
 SMALL = 256
-ZF_COLS = 1152
+ZF_COLS = 1280
 
 
 def nn(a, b):
@@ -48,20 +48,27 @@
 N_SEND, N_RECV, N_LOCAL = 128, 192, 64
 
 SCHEDULE = {
-    "dhA": (("end", (1, 0)), ("mid", (0, 2)),),
-    "dnD": (("mid", (0, 0)),),
-    "nb0": (("end", (3, 0)), ("end", (1, 2)), ("end", (2, 1)),),
-    "nb1": (("mid", (0, 1)), ("mid", (3, 0)),),
-    "cb": (("end", (2, 0)), ("mid", "pair"),),
-    "tail": (("end", (3, 1)), ("mid", (2, 2)), ("mid", (1, 0)),),
-    "gc2": (("mid", (2, 0)), ("mid", (1, 1)), ("mid", (3, 1)),),
-    "gc3": (("mid", (1, 2)), ("mid", (3, 2)),),
-    "blk1": (("end", (1, 1)),),
-    "blk3": (("mid", (2, 1)), ("mid", "pair sum"), ("mid", (4, 0)), ("mid", (1, 3)), ("mid", (4, 2)),),
-    "dt0": (("end", (4, 0)), ("end", (4, 1)), ("end", (3, 2)), ("end", (2, 2)), ("end", (1, 3)),),
-    "dt1": (("end", "pair"), ("mid", (4, 1)), ("mid", (2, 3)),),
-    "dt3": (("end", (4, 2)), ("end", (2, 3)), ("end", (3, 3)), ("mid", (3, 3)),),
-    "sm": (("end", (4, 3)), ("end", "pair sum"), ("mid", (4, 3)),),
+    "dhA": (("end", (1, 1)), ("end", (1, 0)), ("mid", (0, 2)), ("mid", (0, 0)),),
+    "dhD": (("mid", "pair"),),
+    "dnA": (("end", (2, 0)),),
+    "dnD": (("end", (3, 0)),),
+    "nb2": (("mid", (2, 0)), ("mid", (1, 0)),),
+    "cb": (("end", (2, 1)), ("mid", (3, 0)), ("mid", (2, 1)),),
+    "d1a": (("mid", (1, 1)), ("mid", (2, 2)),),
+    "tail": (("end", (3, 1)),),
+    "d1b": (("mid", (0, 1)),),
+    "gc1": (("end", (3, 2)), ("end", (1, 3)), ("mid", (3, 1)),),
+    "gc2": (("end", (4, 0)), ("end", (1, 2)),),
+    "gc3": (("mid", (1, 2)),),
+    "blk0": (("end", (4, 1)), ("end", "pair"),),
+    "blk1": (("mid", (4, 0)), ("mid", (1, 3)),),
+    "blk2": (("end", (2, 2)),),
+    "blk3": (("mid", (3, 2)), ("mid", (4, 1)),),
+    "dt0": (("end", (2, 3)),),
+    "dt1": (("end", (4, 2)),),
+    "dt2": (("mid", (4, 2)), ("mid", "pair sum"), ("mid", (2, 3)),),
+    "dt3": (("mid", (3, 3)),),
+    "sm": (("end", (3, 3)), ("end", (4, 3)), ("end", "pair sum"), ("mid", (4, 3)),),
 }
 
 
@@ -344,12 +351,22 @@
     s_h2, r_h2 = take_s(NCH), take_r(NCH)
     ld_wg.wait()
     ld_wu.wait()
-    NF = FW // 256
+    NF, NA = FW // 256, ZF_COLS // 256
     overlap = 2 * FW - FL
     col_iota = lax.broadcasted_iota(jnp.int32, (2 * ROWS_CHUNK, 256), 1)
 
     def sent(n):
         return (n // CPS) * CPS + (CPS - 1 - n % CPS)
+
+    def ffn_tile(h, cols, keep):
+        g = nn(h, wg_v[:, cols])
+        u = nn(h, wu_v[:, cols])
+        sg = jax.nn.sigmoid(g)
+        si = g * sg
+        slope = u * sg * (1.0 + g * (1.0 - sg))
+        if keep is not None:
+            si, slope = jnp.where(keep, si, 0.0), jnp.where(keep, slope, 0.0)
+        return (si * u).astype(BF), slope.astype(BF), si.astype(BF)
 
     def residual_chunk(k):
         rows = pl.ds(pl.multiple_of(k * ROWS_CHUNK, ROWS_CHUNK), ROWS_CHUNK)
@@ -372,19 +389,18 @@
         def tile(j, _):
             cols = pl.ds(pl.multiple_of(j * 256, 256), 256)
             h = h2_v[:, rows, :].reshape(2 * ROWS_CHUNK, D)
-            g = nn(h, wg_v[:, cols])
-            u = nn(h, wu_v[:, cols])
             keep = col_iota + j * 256 >= c * overlap
-            sg = jax.nn.sigmoid(g)
-            si = jnp.where(keep, g * sg, 0.0)
-            shape = (2, ROWS_CHUNK, 256)
-            hid[:, rows, cols] = (si * u).astype(BF).reshape(shape)
-            slope = jnp.where(keep, u * sg * (1.0 + g * (1.0 - sg)), 0.0)
-            dg[:, rows, cols] = slope.astype(BF).reshape(shape)
-            du[:, rows, cols] = si.astype(BF).reshape(shape)
+            for ref, v in zip((hid, dg, du), ffn_tile(h, cols, keep)):
+                ref[:, rows, cols] = v.reshape(2, ROWS_CHUNK, 256)
             return 0
 
-        lax.fori_loop(0, NF, tile, 0, unroll=True)
+        lax.fori_loop(0, NA, tile, 0, unroll=True)
+
+    def forward_rest(slot):
+        for j in range(NA, NF):
+            cols = slice(j * 256, (j + 1) * 256)
+            for ref, v in zip((hid, dg, du), ffn_tile(h2_v[slot], cols, None)):
+                ref[slot, :, cols] = v
 
     for sub in range(SUBS):
         w_far(sub)
@@ -470,47 +486,65 @@
 
     def g_block(lhs_ref, rhs_ref, zp, pair, parts=(0, 1)):
         lhs = lhs_ref[:, :, pl.ds(pl.multiple_of(zp * GR, GR), GR)].reshape(2 * R, GR)
-        cut = -(-FW // 512) * 256
+        cut = ZF_COLS
         for n in parts:
             cols = slice(0, cut) if n == 0 else slice(cut, FW)
             v = tn(lhs, rhs_ref[:, :, cols].reshape(2 * R, cols.stop - cols.start)).astype(BF)
             outs[2 * pair, :, cols] = v[:SR]
             outs[2 * pair + 1, :, cols] = v[SR:]
 
-    def down_copies(zp, pair):
+    def line_copies(u):
+        zp = order(u)
         return [
-            cp
+            local(outs.at[2 * (u % 2) + h, :, pl.ds(0, ZF_COLS)], gb0.at[zp, h], l_g + 2 * (u % 2) + h)
             for h in range(2)
-            for cp in (
-                local(outs.at[2 * pair + h, :, pl.ds(0, ZF_COLS)], gb0.at[zp, h], l_g + 4 * pair + 2 * h),
-                local(
-                    outs.at[2 * pair + h, :, pl.ds(ZF_COLS, FW - ZF_COLS)],
-                    gb1.at[zp, h], l_g + 4 * pair + 2 * h + 1,
-                ),
+        ]
+
+    def pair_copies(u):
+        zp = order(u)
+        return [
+            local(
+                outs.at[2 * (u % 2) + h, :, pl.ds(ZF_COLS, FW - ZF_COLS)],
+                gb1.at[zp, h], l_g + 4 + 2 * (u % 2) + h,
             )
+            for h in range(2)
         ]
 
-    def down_sends(u):
-        zp = order(u)
-        for cp in down_copies(zp, u % 2):
+    def start(copies):
+        for cp in copies:
+            cp.start()
+
+    def wait(copies):
+        for cp in copies:
             cp.wait()
+
+    def line_sends(u):
+        wait(line_copies(u))
         if u < NZ - 1:
 
             @pl.when(end)
             def _():
                 for h in range(2):
-                    z_send(0, gb0.at[zp, h], u, zp, h)
-
-            y_send(1, u)
+                    z_send(0, gb0.at[order(u), h], u, order(u), h)
+
+    def pair_sends(u):
+        wait(pair_copies(u))
+        y_send(1, u)
 
     for u in range(NZ):
         g_block(dy_v, hid, order(u), u % 2, (0,))
+        start(line_copies(u))
+        if u == 0:
+            forward_rest(0)
+            line_sends(0)
+            forward_rest(1)
+        else:
+            pair_sends(u - 1)
+        g_block(dy_v, hid, order(u), u % 2, (1,))
+        start(pair_copies(u))
         if u > 0:
-            down_sends(u - 1)
-        g_block(dy_v, hid, order(u), u % 2, (1,))
-        for cp in down_copies(order(u), u % 2):
-            cp.start()
-    down_sends(NZ - 1)
+            line_sends(u)
+    pair_sends(NZ - 1)
 
     ld_wd.wait()
 
@@ -638,12 +672,13 @@
         else:
             srcs = [(gbs[j].at[z, h], None)]
         if role == "mid":
-            return srcs + [from_line(j, 0, z, h), from_line(j, 1, z, h)]
+            near = jnp.where(z < NZ // 2, 0, 1)
+            return srcs + [from_line(j, 1 - near, z, h), from_line(j, near, z, h)]
         return srcs + [from_line(j, jnp.where(z == 0, 1, 0), z, h)]
 
     def swap_pieces(j):
         if j == 4:
-            return [(None, m * CH, CH, g_conv.at[m], c * CH) for m in range(4)]
+            return [(None, 0, 4 * CH, g_conv.at[c], 0)]
         mat = g_ffn.at[{0: 0, 1: 0, 2: 1, 3: 2}[j]]
         w = widths[j]
         if j == 1:
@@ -876,6 +911,7 @@
         send_dhalo.start()
 
     y_send(3, 2)
+    y_send(2, 3)
 
     hook("cb")
 
@@ -974,7 +1010,7 @@
         return 0
 
     chunks("gc", NZ, g_mixer)
-    for j in (1, 2, 3, 4):
+    for j in (3, 4):
         y_send(j, NZ - 1)
 
     l_o = take_l(2)
@@ -1036,6 +1072,33 @@
         sm_t[q] = jnp.where(is_gain, gains, tap_sums)
     for k, dev in others:
         remote(sm_t.at[dev[0] // 2], sm_r.at[k], s_sm + k, r_sm + k, dev).start()
+    @pl.when(end)
+    def _():
+        for e in range(NZ - 1):
+            for h in range(2):
+                per_core(0, lambda cut: wait_send(cut(gb0.at[0, h]), s_z[0] + 2 * e + h))
+
+    for j in range(1, 5):
+        for u in range(NZ - 1):
+            per_core(j, lambda cut: wait_send(cut(ybs[j].at[0]), s_y[j] + u))
+    for q in range(S):
+        h1_send(q).wait_send()
+    for k in range(NCH):
+        wait_send(h2_v.at[0, pl.ds(k * ROWS_CHUNK, ROWS_CHUNK)], s_do + k)
+        wait_send(ring.at[k], s_x1 + k)
+        wait_send(ring.at[4 + k], s_xdn + k)
+    for cp in dp_sends:
+        cp.wait_send()
+
+    @pl.when(has_next)
+    def _():
+        for q in range(S):
+            halo_send(q).wait_send()
+
+    @pl.when(has_prev)
+    def _():
+        send_dhalo.wait_send()
+
     hook("sm")
 
     total = sm_t[s // 2]
@@ -1057,33 +1120,9 @@
                 if finish is not None:
                     finish()
 
-    @pl.when(end)
-    def _():
-        for e in range(NZ - 1):
-            for h in range(2):
-                per_core(0, lambda cut: wait_send(cut(gb0.at[0, h]), s_z[0] + 2 * e + h))
-
     for j in range(1, 5):
-        for u in range(NZ):
-            per_core(j, lambda cut: wait_send(cut(ybs[j].at[0]), s_y[j] + u))
+        per_core(j, lambda cut: wait_send(cut(ybs[j].at[0]), s_y[j] + NZ - 1))
     per_core(0, lambda cut: wait_send(cut(yb0), s_f0))
-    for q in range(S):
-        h1_send(q).wait_send()
-    for k in range(NCH):
-        wait_send(h2_v.at[0, pl.ds(k * ROWS_CHUNK, ROWS_CHUNK)], s_do + k)
-        wait_send(ring.at[k], s_x1 + k)
-        wait_send(ring.at[4 + k], s_xdn + k)
-    for cp in dp_sends:
-        cp.wait_send()
-
-    @pl.when(has_next)
-    def _():
-        for q in range(S):
-            halo_send(q).wait_send()
-
-    @pl.when(has_prev)
-    def _():
-        send_dhalo.wait_send()
 
 
 def fused_body(tokens, gain_mix, w_in, kernel, w_out, gain_ffn, w_gate, w_up, w_down, cotangent):
@@ -1103,7 +1142,7 @@
     def sds(shape, dtype=BF):
         return jax.ShapeDtypeStruct(shape, dtype)
 
-    outs = [sds((R, D)), sds((R, D)), sds((3, DR, FL)), sds((4, DR, CL)), sds((8, SMALL), F32)]
+    outs = [sds((R, D)), sds((R, D)), sds((3, DR, FL)), sds((2, DR, 2 * CL)), sds((8, SMALL), F32)]
     outs += [sds((NZ, 2, SR, w)) for w in widths]
     outs += [sds((SR, widths[0]))] + [sds((NZ, SR, w)) for w in widths[1:]]
     outs += [sds((2, NZ, 2, SR, widths[0]))] + [sds((2, NZ, SR, w)) for w in widths[1:]]
@@ -1185,7 +1224,7 @@
     block_v, d_v, ffn, conv, small, gate_v, up_v, down_v, in_v, out_v, mix_v, taps_v, gain_v, sem,
 ):
     D = d_in.shape[1]
-    CL = conv_in.shape[2]
+    CL = conv_in.shape[2] // 2
     s = lax.axis_index("seq")
     count = [0]
 
@@ -1203,9 +1242,13 @@
     down_v[...] = ffn[0].astype(F32)
     stores.append(copy(down_v, g_down))
     loads[1].wait()
-    in_v[...] = conv[0:3].astype(F32)
+    half = CL // 2
+    for core in range(2):
+        for m in range(3):
+            in_v[m, :, core * half : (core + 1) * half] = conv[core, :, m * half : (m + 1) * half].astype(F32)
     stores.append(copy(in_v, g_in))
-    out_v[...] = conv[3].astype(F32)
+    for core in range(2):
+        out_v[:, core * half : (core + 1) * half] = conv[core, :, 3 * half : 4 * half].astype(F32)
     stores.append(copy(out_v, g_out))
     passing[0].wait()
     stores.append(copy(block_v, block_out))
@@ -1233,7 +1276,7 @@
 def finish(n_seq, block_out, d_tokens, g_ffn, g_conv, small):
     R, D = block_out.shape
     _, DR, FL = g_ffn.shape
-    CL = g_conv.shape[2]
+    CL = g_conv.shape[2] // 2
     any_spec = pl.BlockSpec(memory_space=pl.ANY)
     V = pltpu.VMEM
     tails = [

time: 258 us -> 255 us (0.988)
  Pallas kernels: 256 us -> 253 us
where the time goes in v2:
time: 255 us; the launch traced here: 254 us
  Pallas kernels  253 us (99%)
    pallas_call x1, Pallas kernels, fused_body(): pl.pallas_call(functools.partial(step_kernel, (R, T, D, CL, FL, FW)), out...  247 us
    pallas_call x1, Pallas kernels, finish(): pl.pallas_call(functools.partial(finish_kernel, n_seq), out_shape=[low, l...  6.22 us

profile of v2, /device:TPU:0, one launch (start us, length us, event | category | flops | bytes accessed | tf_op | source)
XLA Modules:
  0.0 254.1 jit_solution(4341292875619094709)
XLA Ops:
  0.6 247.1 %block_step.1 = (bf16[512,1536]{1,0:T(8,128)(2,1)}, bf16[512,1536]{1,0:T(8,128)(2,1)}, bf16[3,96,3456]{2,1,0:T(8,128)(2,1)}, bf16[2,96,1536]{2,1,0:T(8,128)(2,1)...) custom-call(bf16[512,1536]{1,0:T(8,128)(2,1)} %bitcast.6, ...), custom_call_target="tpu_custom_call" | custom-call | flops 63417876480 | bytes 209715200 | tf_op jit(solution)/shard_map/block_step/pallas_call | solution.py:1196
  247.7 6.2 %finish.1 = (bf16[512,1536]{1,0:T(8,128)(2,1)}, bf16[512,1536]{1,0:T(8,128)(2,1)}, f32[96]{0:T(128)}, f32[3,96,768]{2,1,0:T(8,128)}, f32[3,1,48]{2,1,0:T(1,128)}...) custom-call(bf16[512,1536]{1,0:T(8,128)(2,1)} %get-tuple-element.25.block_, ...), custom_call_target="tpu_custom_call" | custom-call | tf_op jit(solution)/shard_map/finish/pallas_call | solution.py:1288

commit v3 on v2

--- a/solution.py
+++ b/solution.py
@@ -48,27 +48,26 @@
 N_SEND, N_RECV, N_LOCAL = 128, 192, 64
 
 SCHEDULE = {
-    "dhA": (("end", (1, 1)), ("end", (1, 0)), ("mid", (0, 2)), ("mid", (0, 0)),),
-    "dhD": (("mid", "pair"),),
-    "dnA": (("end", (2, 0)),),
-    "dnD": (("end", (3, 0)),),
-    "nb2": (("mid", (2, 0)), ("mid", (1, 0)),),
-    "cb": (("end", (2, 1)), ("mid", (3, 0)), ("mid", (2, 1)),),
-    "d1a": (("mid", (1, 1)), ("mid", (2, 2)),),
-    "tail": (("end", (3, 1)),),
-    "d1b": (("mid", (0, 1)),),
-    "gc1": (("end", (3, 2)), ("end", (1, 3)), ("mid", (3, 1)),),
-    "gc2": (("end", (4, 0)), ("end", (1, 2)),),
-    "gc3": (("mid", (1, 2)),),
-    "blk0": (("end", (4, 1)), ("end", "pair"),),
-    "blk1": (("mid", (4, 0)), ("mid", (1, 3)),),
-    "blk2": (("end", (2, 2)),),
-    "blk3": (("mid", (3, 2)), ("mid", (4, 1)),),
-    "dt0": (("end", (2, 3)),),
-    "dt1": (("end", (4, 2)),),
-    "dt2": (("mid", (4, 2)), ("mid", "pair sum"), ("mid", (2, 3)),),
-    "dt3": (("mid", (3, 3)),),
-    "sm": (("end", (3, 3)), ("end", (4, 3)), ("end", "pair sum"), ("mid", (4, 3)),),
+    "dhA": (("end", (2, 0)), ("mid", (0, 0)), ("mid", (0, 2)),),
+    "dhD": (("end", (1, 0)),),
+    "dnA": (("mid", "pair"),),
+    "nb0": (("end", (1, 2)),),
+    "nb1": (("mid", (2, 0)),),
+    "nb2": (("end", (3, 0)),),
+    "nb3": (("end", (2, 1)),),
+    "cb": (("end", (3, 1)),),
+    "d1a": (("end", (2, 2)), ("mid", (1, 0)), ("mid", (0, 1)), ("mid", (3, 0)),),
+    "tail": (("mid", (1, 1)),),
+    "d1b": (("mid", (2, 2)),),
+    "gc1": (("end", "pair"),),
+    "gc3": (("end", (1, 3)), ("end", (1, 1)), ("end", (4, 0)), ("end", (4, 1)),),
+    "blk0": (("mid", (3, 2)),),
+    "blk1": (("mid", (2, 3)), ("mid", (1, 2)),),
+    "blk3": (("end", (3, 2)), ("mid", (2, 1)),),
+    "dt0": (("mid", (4, 0)), ("mid", (1, 3)), ("mid", (3, 1)), ("mid", (4, 1)), ("mid", (4, 2)),),
+    "dt1": (("end", (2, 3)), ("end", (4, 2)), ("end", "pair sum"),),
+    "dt2": (("end", (3, 3)),),
+    "sm": (("end", (4, 3)), ("mid", "pair sum"), ("mid", (3, 3)), ("mid", (4, 3)),),
 }
 
 

time: 255 us -> 254 us (level)
  no operation moved by 1% of the time
where the time goes in v3:
time: 254 us; the launch traced here: 253 us
  Pallas kernels  252 us (99%)
    pallas_call x1, Pallas kernels, fused_body(): pl.pallas_call(functools.partial(step_kernel, (R, T, D, CL, FL, FW)), out...  246 us
    pallas_call x1, Pallas kernels, finish(): pl.pallas_call(functools.partial(finish_kernel, n_seq), out_shape=[low, l...  6.22 us

profile of v3, /device:TPU:0, one launch (start us, length us, event | category | flops | bytes accessed | tf_op | source)
XLA Modules:
  0.0 252.7 jit_solution(7716780698373001878)
XLA Ops:
  0.6 245.6 %block_step.1 = (bf16[512,1536]{1,0:T(8,128)(2,1)}, bf16[512,1536]{1,0:T(8,128)(2,1)}, bf16[3,96,3456]{2,1,0:T(8,128)(2,1)}, bf16[2,96,1536]{2,1,0:T(8,128)(2,1)...) custom-call(bf16[512,1536]{1,0:T(8,128)(2,1)} %bitcast.6, ...), custom_call_target="tpu_custom_call" | custom-call | flops 63417876480 | bytes 209715200 | tf_op jit(solution)/shard_map/block_step/pallas_call | solution.py:1195
  246.3 6.2 %finish.1 = (bf16[512,1536]{1,0:T(8,128)(2,1)}, bf16[512,1536]{1,0:T(8,128)(2,1)}, f32[96]{0:T(128)}, f32[3,96,768]{2,1,0:T(8,128)}, f32[3,1,48]{2,1,0:T(1,128)}...) custom-call(bf16[512,1536]{1,0:T(8,128)(2,1)} %get-tuple-element.25.block_, ...), custom_call_target="tpu_custom_call" | custom-call | tf_op jit(solution)/shard_map/finish/pallas_call | solution.py:1287
